TPU v7x, 32 devices: a whole 2x2x4 slice. The times are simulated.
32 devices in a mesh: groups: 2 (over x), row: 4 (over y, core), col: 4 (over z).
Axes of the slice: x: 2, y: 2, z: 4, core: 2. Of those that a mesh axis runs over, the one named last changes fastest.
Arguments:
- zroot: float32 [4096, 2048], P(('groups', 'row')), parts along dimension 0, as said below
- panel_one: float32 [8, 2048, 1024], P(('groups', 'col'), 'row'), parts along dimension 0, may hold values from -0.125 to 0.125
- inv_one: float32 [8, 1024, 1024], P(('groups', 'col')), parts along dimension 0
- panel_two_j: float32 [16, 1024, 512], P(('groups', 'col'), 'row'), parts along dimension 0, may hold values from -0.109375 to 0.109375
- panel_two_r: float32 [16, 2048, 512], P(('groups', 'col'), 'row'), parts along dimension 0, may hold values from -0.109375 to 0.109375
- inv_two: float32 [16, 512, 512], P(('groups', 'col')), parts along dimension 0
- parents: int32 [16], P(('groups', 'col')), parts along dimension 0, may hold values from 0 to 3
- widths: int32 [16], P(('groups', 'col')), parts along dimension 0, may hold values from 256 to 512, as said below
- pattern_j: int32 [16, 16], P(('groups', 'col'), 'row'), parts along dimension 0, may hold values 0 or 1
- pattern_r: int32 [16, 32], P(('groups', 'col'), 'row'), parts along dimension 0, may hold values 0 or 1
Outputs:
- var_one: float32 [8, 1024], P(('groups', 'col'), 'row'), parts along dimension 0
- var_two: float32 [16, 512], P(('groups', 'col'), 'row'), parts along dimension 0
- z_two_j: float32 [16, 1024, 512], P(('groups', 'col'), 'row'), parts along dimension 0
- z_two_r: float32 [16, 2048, 512], P(('groups', 'col'), 'row'), parts along dimension 0
There are 2 independent parts, one for each index of `groups`. A program takes and returns all parts, laid end to end along the dimension named above; each array names one. Nothing has to cross between parts.
Inputs may be any that keep to these rules, and one draw needn't show every extreme that they name: zroot is symmetric: it equals its transpose up to rounding, as a selected inverse block of a symmetric matrix does. `widths`: the live width of each level-2 supernode; columns at or past it are padding. `parents`: index of the level-1 parent of each level-2 supernode. `pattern_j`: 1 where a tile of 64 rows of the panel is stored. `pattern_r`: 1 where a tile of 64 rows of the panel is stored.
All inputs are finite; a program needn't handle non-finite values. No bound on the sum of `pattern_j` or of `pattern_r` on one device may be relied on, other than what follows from the above.
Results may differ from a plain program's by a relative error of at most 0.0003.
Values sent between devices are 32-bit elements; how exact they have to be, the bound alone decides.
A program may use at most 128 MiB of HBM per device.

v0:
```python
import functools

import jax
import jax.numpy as jnp
from jax import lax
from jax.experimental import pallas as pl
from jax.experimental.pallas import tpu as pltpu
from jax.sharding import PartitionSpec as P

TILE = 64
PRECISION = lax.Precision.HIGH


def product(left, right):
    return jnp.dot(left, right, precision=PRECISION, preferred_element_type=jnp.float32)


def crossed(left, right):
    return lax.dot_general(
        left, right, (((0,), (0,)), ((), ())), precision=PRECISION, preferred_element_type=jnp.float32
    )


def swap(block, bit):
    n = lax.axis_size("row")
    return lax.ppermute(block, "row", [(i, i ^ bit) for i in range(n)])


def own_first(array, axis):
    n = lax.axis_size("row")
    me = lax.axis_index("row")
    share = array.shape[axis] // n
    pieces = [
        lax.dynamic_slice_in_dim(array, (me ^ d) * share, share, axis) for d in range(n)
    ]
    return jnp.concatenate(pieces, axis)


def row_blocks(block):
    n = lax.axis_size("row")
    held = {0: block}
    bit = n // 2
    while bit:
        for d in sorted(held):
            held[d | bit] = swap(held[d], bit)
        bit //= 2
    return [held[d] for d in range(n)]


def row_sum(pieces):
    n = lax.axis_size("row")
    held = dict(enumerate(pieces))
    bit = 1
    while bit < n:
        for d in [d for d in sorted(held) if not d & bit]:
            held[d] = held[d] + swap(held.pop(d | bit), bit)
        bit *= 2
    return held[0]


def reordered(block, d):
    n = lax.axis_size("row")
    share = block.shape[1] // n
    return jnp.concatenate(
        [block[:, (d ^ e) * share : ((d ^ e) + 1) * share] for e in range(n)], 1
    )


def general_body(
    zroot,
    panel_one,
    inv_one,
    panel_two_j,
    panel_two_r,
    inv_two,
    parents,
    widths,
    pattern_j,
    pattern_r,
):
    n = lax.axis_size("row")
    width_one = inv_one.shape[1]
    node_rows = width_one // n
    nodes, width_two = inv_two.shape[:2]
    root_rows = zroot.shape[0]

    inverse = own_first(inv_one[0], 1)
    factor = product(panel_one[0], inverse)
    all_factors = lax.all_gather(factor, "col", axis=0)
    gram = crossed(inverse[:, :node_rows], inverse)
    factor_tied, gram = lax.optimization_barrier((factor, gram))
    all_grams = lax.all_gather(gram, "col", axis=0)

    live = (jnp.arange(width_two)[None, :] < widths[:, None]).astype(jnp.float32)
    mask_j = jnp.repeat(pattern_j.astype(jnp.float32), TILE, axis=1)
    mask_r = jnp.repeat(pattern_r.astype(jnp.float32), TILE, axis=1)
    factor_j = []
    factor_r = []
    for i in range(nodes):
        masked_j = panel_two_j[i] * mask_j[i][:, None] * live[i][None, :]
        masked_r = panel_two_r[i] * mask_r[i][:, None] * live[i][None, :]
        factor_j.append(product(masked_j, inv_two[i]))
        factor_r.append(product(masked_r, inv_two[i]))
    near_j = jnp.concatenate(factor_j, 1)
    full_j = jnp.concatenate(row_blocks(near_j), 0)

    root = own_first(zroot, 1)
    full_factor = jnp.concatenate(
        [reordered(block, d) for d, block in enumerate(row_blocks(factor))], 0
    )
    image = product(root, full_factor)
    terms = jnp.sum(factor * image, axis=0).reshape(n, node_rows)
    own_squares = jnp.sum(inverse[:, :node_rows] ** 2, axis=0)
    var_one = (own_squares + row_sum([terms[d] for d in range(n)]))[None, :]

    all_factors, var_one = lax.optimization_barrier((all_factors, var_one))

    parent_factor = [
        lax.dynamic_index_in_dim(all_factors, parents[i], 0, False) for i in range(nodes)
    ]
    reduced = [
        factor_r[i] - product(parent_factor[i], full_j[:, i * width_two : (i + 1) * width_two])
        for i in range(nodes)
    ]
    block_r = []
    sums_j = []
    for i in range(nodes):
        block_r.append(-product(root, jnp.concatenate(row_blocks(reduced[i]), 0)))
        upper = crossed(parent_factor[i], block_r[i]).reshape(n, node_rows, width_two)
        sums_j.append(row_sum([upper[d] for d in range(n)]))
    block_j = []
    for i in range(nodes):
        parent_gram = lax.dynamic_index_in_dim(all_grams, parents[i], 0, False)
        near = product(parent_gram, full_j[:, i * width_two : (i + 1) * width_two])
        block_j.append(-(near + sums_j[i]))

    corrections = jnp.stack(
        [
            jnp.sum(factor_j[i] * block_j[i], axis=0) + jnp.sum(factor_r[i] * block_r[i], axis=0)
            for i in range(nodes)
        ]
    )
    share = width_two // n
    me = lax.axis_index("row")
    ordered = own_first(corrections, 1).reshape(nodes, n, share)
    summed = row_sum([ordered[:, d] for d in range(n)])
    squares = jnp.sum(inv_two * inv_two, axis=1)
    live_share = lax.dynamic_slice_in_dim(live, me * share, share, 1)
    square_share = lax.dynamic_slice_in_dim(squares, me * share, share, 1)
    var_two = live_share * (square_share - summed)
    return (var_one, var_two, jnp.stack(block_j), jnp.stack(block_r))


PIECE = 16
RING = 16
AHEAD = 8
STEP = 128


def mm(left, right):
    return jnp.dot(left, right, precision=PRECISION, preferred_element_type=jnp.float32)


def mm_t(left, right):
    return lax.dot_general(
        left, right, (((0,), (0,)), ((), ())), precision=PRECISION, preferred_element_type=jnp.float32
    )


def line_kernel(
    parents,
    widths,
    tiles_j,
    tiles_r,
    zroot,
    panel_one,
    inv_one,
    panel_j,
    panel_r,
    inv_two,
    var_one,
    var_two,
    z_j,
    z_r,
    root,
    own,
    near_j,
    near_r,
    part_out,
    part_own,
    held,
    staged,
    full_j,
    chosen,
    reduced,
    across,
    beside,
    part_in,
    part_y,
    note,
    vec_a,
    vec_b,
    loads,
    note_send,
    note_recv,
    line_send,
    line_recv,
    j_send,
    j_recv,
    g_send,
    g_recv,
    r_send,
    r_recv,
    u_send,
    u_recv,
    a_send,
    a_recv,
    b_send,
    b_recv,
):
    rows = root.shape[0]
    width = own.shape[1]
    node = near_j.shape[0]
    nodes, _, two = z_r.shape
    chunks = own.shape[0] // PIECE
    steps = rows // STEP
    per = STEP // PIECE
    half = width // 2

    z = lax.axis_index("col")
    r = lax.axis_index("row")
    core = r % 2
    side = r // 2
    twin = r + 1 - 2 * core
    over = (r + 2) % 4
    diag = (twin + 2) % 4
    inner = jnp.logical_or(z == 1, z == 2)
    outer = jnp.logical_not(inner)

    def remote(src, dst, send, recv, device):
        return pltpu.make_async_remote_copy(
            src_ref=src,
            dst_ref=dst,
            send_sem=send,
            recv_sem=recv,
            device_id=device,
            device_id_type=pl.DeviceIdType.MESH,
        )

    def at_row(index):
        return (lax.axis_index("groups"), index, z)

    def at_col(index):
        return (lax.axis_index("groups"), r, index)

    def span(index, size):
        return pl.ds(pl.multiple_of(index * size, size), size)

    def child(m):
        return pl.ds(m * two, two)

    def load(k):
        if k == 0:
            return pltpu.make_async_copy(panel_one.at[0], own.at[pl.ds(0, rows)], loads.at[0])
        if k < 3:
            h = k - 1
            return pltpu.make_async_copy(inv_one.at[0, pl.ds(h * half, half)], chosen.at[h], loads.at[k])
        if k < 5:
            m = k - 3
            return pltpu.make_async_copy(panel_j.at[m], near_j.at[:, child(m)], loads.at[k])
        if k == 5:
            return pltpu.make_async_copy(inv_two, part_in, loads.at[5])
        if k < 8:
            m = k - 6
            return pltpu.make_async_copy(panel_r.at[m], near_r.at[:, child(m)], loads.at[k])
        return pltpu.make_async_copy(zroot, root, loads.at[8])

    for k in range(3):
        load(k).start()

    barrier = pltpu.get_barrier_semaphore()

    def greet(device):
        pl.semaphore_signal(barrier, inc=1, device_id=device, device_id_type=pl.DeviceIdType.MESH)

    for peer in (twin, over, diag):
        greet(at_row(peer))

    @pl.when(outer)
    def _():
        greet(at_col(1 + z // 3))

    @pl.when(inner)
    def _():
        greet(at_col(3 - z))
        greet(at_col(((z - 1) * 3) % 4))

    low = z < 2
    place = jnp.where(low, z, 3 - z)
    kin = [jnp.where(low, parents[m], 3 - parents[m]) for m in range(nodes)]
    picks = [
        jnp.where(place == 1, (kin[m] + 3) % 4, jnp.where(kin[m] == 0, 0, 1 + m)) for m in range(nodes)
    ]
    note[0] = jnp.zeros(note.shape[1:], jnp.int32)
    for m in range(nodes):
        note[0, m : m + 1, :] = jnp.full((1, width), kin[m], jnp.int32)

    @pl.when(outer)
    def _():
        pl.semaphore_wait(barrier, 4)

    @pl.when(inner)
    def _():
        pl.semaphore_wait(barrier, 5)

    def note_copy():
        return remote(note.at[0], note.at[1], note_send, note_recv, at_col(1 + z // 3))

    @pl.when(outer)
    def _():
        note_copy().start()

    def line(stream, t):
        at = span(t, PIECE)
        if stream == 0:
            src, dst, device = own.at[at], held.at[2, at], at_col(1 + z // 3)
        elif stream == 1:
            src, dst, device = own.at[at], held.at[0, at], at_col(3 - z)
        elif stream == 2:
            src, dst, device = held.at[2, at], held.at[1, at], at_col(3 - z)
        else:
            src = staged.at[stream - 3, span(t % RING, PIECE)]
            dst, device = held.at[stream - 3, at], at_col(((z - 1) * 3) % 4)
        return remote(src, dst, line_send.at[stream, t], line_recv.at[stream, t], device)

    def to_inner(first, last):
        @pl.when(outer)
        def _():
            def go(t, carry):
                line(0, t).start()
                return carry

            lax.fori_loop(first, last, go, 0)

    def forward(t):
        line(0, t).wait_recv()
        line(2, t).start()

    def chunk(t):
        @pl.when(inner)
        def _():
            @pl.when(t + AHEAD < chunks)
            def _():
                line(1, t + AHEAD).start()
                forward(t + AHEAD)

            line(1, t).wait_recv()
            line(2, t).wait_recv()
            at = span(t, PIECE)
            for m in range(nodes):
                pick = note[1, m : m + 1, :]

                @pl.when(t >= RING)
                def _():
                    line(3 + m, t - RING).wait_send()

                staged[m, span(t % RING, PIECE), :] = jnp.where(
                    pick < 2, own[at, :], jnp.where(pick == 2, held[0, at, :], held[1, at, :])
                )
                line(3 + m, t).start()

        @pl.when(outer)
        def _():
            line(3, t).wait_recv()
            line(4, t).wait_recv()

    def j_copy(k):
        mine = span(r, node)
        theirs = span(over, node)
        if k == 2:
            return remote(full_j.at[theirs], full_j.at[theirs], j_send.at[2], j_recv.at[2], at_row(twin))
        return remote(near_j, full_j.at[mine], j_send.at[k], j_recv.at[k], at_row(over if k == 0 else twin))

    def g_copy(k):
        if k == 4:
            at = pl.ds(0, rows)
            columns = span(1 - core, half)
            return remote(own.at[at, columns], beside, g_send.at[4], g_recv.at[4], at_row(twin))
        top = pl.ds(k // 2 * (rows // 2), rows // 2)
        at = pl.ds(pl.multiple_of(core * rows + k // 2 * (rows // 2), rows // 2), rows // 2)
        if k % 2 == 0:
            columns = span(1 - side, half)
            return remote(own.at[top, columns], across.at[at], g_send.at[k], g_recv.at[k], at_row(over))
        return remote(across.at[at], across.at[at], g_send.at[k], g_recv.at[k], at_row(twin))

    spans = [(k * STEP, STEP) for k in range(steps - 1)]
    spans += [((steps - 1) * STEP, STEP // 2), ((steps - 1) * STEP + STEP // 2, STEP // 2)]

    def r_copy(k, part):
        first, size = spans[part]
        who = over if k == 2 else r
        at = pl.ds(pl.multiple_of(who * rows + first, size), size)
        return remote(
            reduced.at[at],
            reduced.at[at],
            r_send.at[k, part],
            r_recv.at[k, part],
            at_row(over if k == 0 else twin),
        )

    def twice(function):
        def go(h, carry):
            function(h)
            return carry

        lax.fori_loop(0, 2, go, 0)

    part_two = two // 2

    def within(m, h):
        return pl.ds(pl.multiple_of(m * two + h * part_two, part_two), part_two)

    def pick_rows(m, at):
        pick = picks[m]
        first = jnp.where(pick == 0, own[at, :], held[0, at, :])
        second = jnp.where(pick == 2, held[1, at, :], held[2, at, :])
        return jnp.where(pick < 2, first, second)

    def reduce_part(part, m):
        first, size = spans[part]
        at = pl.ds(first, size)
        to = pl.ds(pl.multiple_of(r * rows + first, size), size)
        chosen[m, at, :] = pick_rows(m, at)

        def go(h):
            columns = within(m, h)
            reduced[to, columns] = near_r[at, columns] - mm(chosen[m, at, :], full_j[:, columns])

        twice(go)
        if m == nodes - 1:
            r_copy(0, part).start()
            r_copy(1, part).start()

    def gather_part(part):
        r_copy(0, part).wait_recv()
        r_copy(2, part).start()

    def root_wait(part):
        r_copy(1, part).wait_recv()
        r_copy(2, part).wait_recv()

    def root_step(step, m):
        places = [pl.ds(pl.multiple_of(d * rows + step * STEP, STEP), STEP) for d in range(4)]

        def go(h):
            columns = within(0, h)
            left = jnp.concatenate([root[:, at] for at in places], 1)
            right = jnp.concatenate([reduced[at, within(m, h)] for at in places], 0)
            z_r[m, :, columns] -= mm(left, right)

        twice(go)

    def to_tile(vec):
        return jnp.concatenate([vec[:, i * 128 : (i + 1) * 128] for i in range(vec.shape[1] // 128)], 0)

    def shared(pieces):
        total = jnp.zeros_like(pieces[0])
        for d, one in enumerate(pieces):
            total = total + jnp.where(r == d, one, 0.0)
        return total

    def to_peers(tile, send, recv):
        return [
            remote(tile.at[0], tile.at[1 + k], send.at[k], recv.at[k], at_row(peer))
            for k, peer in enumerate((twin, over, diag))
        ]

    def colsum(left, right):
        return jnp.sum(left * right, axis=0, keepdims=True)

    def factor(first, size):
        at = pl.ds(first, size)
        own[at, :] = mm(own[at, 0:half], chosen[0]) + mm(own[at, half:width], chosen[1])

    def masked(panel, tiles, at, m, first, count):
        column = lax.broadcasted_iota(jnp.int32, (1, two), 1)
        live = (column < widths[m]).astype(jnp.float32)
        blocks = [
            panel[pl.ds(at + i * TILE, TILE), child(m)] * (live * tiles[m, first + i].astype(jnp.float32))
            for i in range(count)
        ]
        return jnp.concatenate(blocks, 0)

    for k in range(3):
        load(k).wait()
    for k in range(3, 9):
        load(k).start()
    factor(0, STEP)
    to_inner(0, per)
    early = 2

    @pl.when(inner)
    def _():
        for t in range(early):
            line(1, t).start()

    for k in range(3, 6):
        load(k).wait()
    for m in range(nodes):
        near_j[:, child(m)] = mm(masked(near_j, tiles_j, 0, m, 0, node // TILE), part_in[m])
    for k in (0, 1):
        j_copy(k).start()

    def pass_on(first, last):
        @pl.when(inner)
        def _():
            for t in range(first, last):
                forward(t)
                if t + early < AHEAD:
                    line(1, t + early).start()

    share = AHEAD // steps
    pass_on(0, share)
    for k in range(1, steps):
        factor(k * STEP, STEP)
        to_inner(k * per, (k + 1) * per)
        pass_on(k * share, (k + 1) * share)
    g_copy(4).start()

    @pl.when(inner)
    def _():
        note_copy().wait_recv()

    full_j[span(r, node), :] = near_j[...]
    for m in range(nodes):
        z_r[m] = jnp.zeros_like(z_r[m])

    def separator_rows(m):
        load(6 + m).wait()

        def go(h):
            size = rows // 2
            at = pl.multiple_of(h * size, size)
            count = size // TILE
            near_r[pl.ds(at, size), child(m)] = mm(masked(near_r, tiles_r, at, m, h * count, count), part_in[m])

        twice(go)

    def gram(k):
        columns = pl.ds(pl.multiple_of(r * node + k * STEP, STEP), STEP)
        own[rows + k * STEP : rows + (k + 1) * STEP, :] = mm_t(chosen[0, :, columns], chosen[0]) + mm_t(
            chosen[1, :, columns], chosen[1]
        )
        to_inner((steps + k) * per, (steps + k + 1) * per)

    one = {}

    def square_sums():
        one["squares"] = sum(
            colsum(chosen[h, :, span(r, node)], chosen[h, :, span(r, node)]) for h in range(2)
        )
        one["squares_two"] = [colsum(part_in[m], part_in[m]) for m in range(nodes)]

    def gathered_j():
        j_copy(0).wait_recv()
        j_copy(2).start()
        j_copy(1).wait_recv()
        j_copy(2).wait_recv()

    def diagonal(h):
        block = own[0:rows, h * half : (h + 1) * half]
        one[h] = colsum(block, mm(root[:, span(r, rows)], block))

    def pair():
        g_copy(4).wait_recv()
        product_two = mm(root[:, span(twin, rows)], beside[...])
        one["pair"] = 2.0 * colsum(own[0:rows, span(core, half)], product_two)

    def cross():
        g_copy(1).wait_recv()
        g_copy(3).wait_recv()
        product_two = mm(root[:, span(1 - side, 2 * rows)], across[...])
        product_two = 2.0 * colsum(own[0:rows, span(side, half)], product_two)
        sums = [
            one[h] + jnp.where(core == h, one["pair"], 0.0) + jnp.where(side == h, product_two, 0.0)
            for h in range(2)
        ]
        vec_a[0] = to_tile(jnp.concatenate(sums, 1))
        for copy in to_peers(vec_a, a_send, a_recv):
            copy.start()

    def level_one_out():
        for copy in to_peers(vec_a, a_send, a_recv):
            copy.wait()
        total = vec_a[0] + vec_a[1] + vec_a[2] + vec_a[3]
        each = total.shape[0] // 4
        mine = shared([total[d * each : (d + 1) * each, :] for d in range(4)])
        var_one[...] = one["squares"] + jnp.concatenate([mine[i : i + 1, :] for i in range(each)], 1)

    def pass_g(k):
        g_copy(k).wait_recv()
        g_copy(k + 1).start()

    def node_step(step, m):
        at = pl.ds(rows + step * STEP, STEP)
        block = pick_rows(m, at)

        def go(h):
            z_j[m, step * STEP : (step + 1) * STEP, within(0, h)] = mm(block, full_j[:, within(m, h)])

        twice(go)

    def upper(m, dest):
        return mm_t(chosen[m, :, span(dest, node)], z_r[m])

    def u_copy(k):
        if k < 2:
            out = part_out.at[pl.ds(k * 2 * node, 2 * node)]
            return remote(out, part_in.at[k], u_send.at[k], u_recv.at[k], at_row(twin))
        out = part_own.at[pl.ds((k - 2) * node, node)]
        return remote(out, part_y.at[k - 2], u_send.at[k], u_recv.at[k], at_row(over))

    def upper_twin(m):
        def go(h):
            at = pl.ds(pl.multiple_of((2 * m + h) * node, node), node)
            part_out[at, :] = upper(m, (twin + 2 - 2 * h) % 4)

        twice(go)
        u_copy(m).start()

    def upper_over(m):
        far = upper(m, over)
        u_copy(m).wait_recv()
        part_own[m * node : (m + 1) * node, :] = far + part_in[m, 0:node, :]
        u_copy(2 + m).start()

    def upper_own(m):
        part_in[m, node : 2 * node, :] = part_in[m, node : 2 * node, :] + upper(m, r)

    def separator_sums():
        one["sums_r"] = [colsum(near_r[:, child(m)], z_r[m]) for m in range(nodes)]

    def item(function, *arguments):
        return functools.partial(function, *arguments)

    work = {
        0: [item(separator_rows, 0)],
        1: [item(separator_rows, 1)],
        2: [item(gram, 0)],
        4: [item(gram, 1)],
        5: [square_sums],
        7: [gathered_j, item(reduce_part, 0, 0)],
        8: [item(reduce_part, 0, 1)],
        9: [load(8).wait, item(diagonal, 0)],
        11: [item(diagonal, 1)],
        14: [item(gather_part, 0), g_copy(0).start],
        15: [item(reduce_part, 1, 0)],
        16: [item(reduce_part, 1, 1)],
        17: [item(root_wait, 0), item(root_step, 0, 0)],
        18: [item(root_step, 0, 1)],
        19: [pair],
        22: [item(pass_g, 0), item(gather_part, 1), g_copy(2).start],
        23: [item(reduce_part, 2, 0)],
        24: [item(reduce_part, 2, 1)],
        25: [item(root_wait, 1), item(root_step, 1, 0)],
        26: [item(root_step, 1, 1)],
        27: [item(reduce_part, 3, 0)],
        28: [item(reduce_part, 3, 1)],
        29: [item(pass_g, 2)],
        30: [item(gather_part, 2)],
        31: [item(reduce_part, 4, 0), item(reduce_part, 4, 1)],
        32: [item(root_wait, 2), item(root_step, 2, 0)],
        33: [item(root_step, 2, 1), item(gather_part, 3)],
        35: [item(gather_part, 4), item(root_wait, 3), item(root_wait, 4), item(root_step, 3, 0)],
        36: [item(upper_twin, 0)],
        37: [item(upper_over, 0), item(root_step, 3, 1)],
        38: [item(upper_twin, 1)],
        39: [item(upper_over, 1)],
        40: [cross],
        41: [item(node_step, 0, 0)],
        42: [item(node_step, 0, 1)],
        43: [item(upper_own, 0)],
        44: [item(upper_own, 1)],
        45: [level_one_out],
        46: [separator_sums],
    }
    done = 0
    for last in sorted(work) + [chunks - 1]:
        if last == done:
            chunk(last)
        else:

            def go(t, carry):
                chunk(t)
                return carry

            lax.fori_loop(done, last + 1, go, 0)
        done = last + 1
        for function in work.get(last, ()):
            function()

    sums_r = one["sums_r"]
    for m in range(nodes):
        node_step(1, m)
    for m in range(nodes):
        u_copy(2 + m).wait_recv()
        z_j[m] = -(z_j[m] + part_in[m, node : 2 * node, :] + part_y[m])
        sums_r[m] = sums_r[m] + colsum(near_j[:, child(m)], z_j[m])
    vec_b[0] = to_tile(jnp.concatenate(sums_r, 1))
    for copy in to_peers(vec_b, b_send, b_recv):
        copy.start()

    @pl.when(outer)
    def _():
        note_copy().wait_send()

        def go(t, carry):
            line(0, t).wait_send()
            return carry

        lax.fori_loop(0, chunks, go, 0)

    @pl.when(inner)
    def _():
        def go(t, carry):
            line(1, t).wait_send()
            line(2, t).wait_send()
            return carry

        lax.fori_loop(0, chunks, go, 0)

        def last(t, carry):
            line(3, t).wait_send()
            line(4, t).wait_send()
            return carry

        lax.fori_loop(chunks - RING, chunks, last, 0)

    for k in range(3):
        j_copy(k).wait_send()
    for k in range(5):
        g_copy(k).wait_send()
    for part in range(len(spans)):
        for k in range(3):
            r_copy(k, part).wait_send()
    for k in range(4):
        u_copy(k).wait_send()
    for copy in to_peers(vec_b, b_send, b_recv):
        copy.wait()
    total = vec_b[0] + vec_b[1] + vec_b[2] + vec_b[3]
    share = two // 4
    column = lax.broadcasted_iota(jnp.int32, (1, share), 1) + r * share
    for m in range(nodes):
        mine = shared([total[m * 4 + d : m * 4 + d + 1, :] for d in range(4)])
        square = shared([one["squares_two"][m][:, d * share : (d + 1) * share] for d in range(4)])
        live = (column < widths[m]).astype(jnp.float32)
        var_two[m : m + 1, :] = live * (square - mine)


def copy_kernel(*refs):
    sems = refs[-1]
    order = (3, 2, 0, 1)
    ins = [pltpu.make_async_copy(refs[k], refs[8 + k], sems.at[k]) for k in order]
    outs = [pltpu.make_async_copy(refs[8 + k], refs[4 + k], sems.at[4 + k]) for k in order]
    for copy in ins:
        copy.start()
    for first, second in zip(ins, outs):
        first.wait()
        second.start()
    for copy in outs:
        copy.wait()


def line_body(
    zroot,
    panel_one,
    inv_one,
    panel_two_j,
    panel_two_r,
    inv_two,
    parents,
    widths,
    pattern_j,
    pattern_r,
):
    n = lax.axis_size("row")
    width = inv_one.shape[1]
    node = width // n
    nodes, two = inv_two.shape[:2]
    rows = zroot.shape[0]
    chunks = (rows + node) // PIECE
    steps = rows // STEP
    f32 = jnp.float32
    smem = pl.BlockSpec(memory_space=pltpu.SMEM)
    hbm = pl.BlockSpec(memory_space=pl.ANY)
    vmem = pl.BlockSpec(memory_space=pltpu.VMEM)
    dma = pltpu.SemaphoreType.DMA
    results = pl.pallas_call(
        line_kernel,
        out_shape=(
            jax.ShapeDtypeStruct((1, node), f32),
            jax.ShapeDtypeStruct((nodes, two // n), f32),
            jax.ShapeDtypeStruct((nodes, node, two), f32),
            jax.ShapeDtypeStruct((nodes, rows, two), f32),
        ),
        in_specs=[smem] * 4 + [hbm] * 6,
        out_specs=(vmem,) * 4,
        scratch_shapes=[
            pltpu.VMEM(zroot.shape, f32),
            pltpu.VMEM((rows + node, width), f32),
            pltpu.VMEM((node, nodes * two), f32),
            pltpu.VMEM((rows, nodes * two), f32),
            pltpu.VMEM((nodes * 2 * node, two), f32),
            pltpu.VMEM((nodes * node, two), f32),
            pltpu.VMEM((3, rows + node, width), f32),
            pltpu.VMEM((nodes, RING * PIECE, width), f32),
            pltpu.VMEM((width, nodes * two), f32),
            pltpu.VMEM((nodes, rows, width), f32),
            pltpu.VMEM((4 * rows, nodes * two), f32),
            pltpu.VMEM((2 * rows, width // 2), f32),
            pltpu.VMEM((rows, width // 2), f32),
            pltpu.VMEM((nodes, 2 * node, two), f32),
            pltpu.VMEM((nodes, node, two), f32),
            pltpu.VMEM((2, 8, width), jnp.int32),
            pltpu.VMEM((4, width // 128, 128), f32),
            pltpu.VMEM((4, nodes * two // 128, 128), f32),
            dma((9,)),
            dma,
            dma,
            dma((5, chunks)),
            dma((5, chunks)),
            dma((3,)),
            dma((3,)),
            dma((5,)),
            dma((5,)),
            dma((3, steps + 1)),
            dma((3, steps + 1)),
            dma((4,)),
            dma((4,)),
            dma((3,)),
            dma((3,)),
            dma((3,)),
            dma((3,)),
        ],
        compiler_params=pltpu.CompilerParams(
            collective_id=0, has_side_effects=True, vmem_limit_bytes=60 * 1024 * 1024
        ),
    )(parents, widths, pattern_j, pattern_r, zroot, panel_one, inv_one, panel_two_j, panel_two_r, inv_two)
    return pl.pallas_call(
        copy_kernel,
        out_shape=tuple(jax.ShapeDtypeStruct(one.shape, one.dtype) for one in results),
        in_specs=[hbm] * 4,
        out_specs=(hbm,) * 4,
        scratch_shapes=[pltpu.VMEM(one.shape, one.dtype) for one in results] + [dma((8,))],
        compiler_params=pltpu.CompilerParams(vmem_limit_bytes=60 * 1024 * 1024),
    )(*results)


def solution(mesh):
    fits = mesh.shape["row"] == 4 and mesh.shape["col"] == 4
    return jax.shard_map(
        line_body if fits else general_body,
        mesh=mesh,
        in_specs=(
            P(("groups", "row"), None),
            P(("groups", "col"), "row", None),
            P(("groups", "col"), None, None),
            P(("groups", "col"), "row", None),
            P(("groups", "col"), "row", None),
            P(("groups", "col"), None, None),
            P(("groups", "col")),
            P(("groups", "col")),
            P(("groups", "col"), "row"),
            P(("groups", "col"), "row"),
        ),
        out_specs=(
            P(("groups", "col"), "row"),
            P(("groups", "col"), "row"),
            P(("groups", "col"), "row", None),
            P(("groups", "col"), "row", None),
        ),
        check_vma=False,
    )
```

profile of v0, /device:TPU:0, one launch (start us, length us, event | category | flops | bytes accessed | tf_op | source)
XLA Modules:
  0.0 173.0 jit_solution(10904574104508305024)
XLA Ops:
  0.6 168.8 %shard_map.129 = (f32[1,256]{1,0:T(1,128)}, f32[2,128]{1,0:T(2,128)}, f32[2,256,512]{2,1,0:T(8,128)}, f32[2,512,512]{2,1,0:T(8,128)}) custom-call(s32[2]{0:T(128)} %parents.1, s32[2]{0:T(128)} %widths.1, s32[2,4]{1,0:T(2,128)} %tiles_j.1, s32[2,8]{1,0:T(2,128)} %tiles_r.1, f32[512,2048]{1,0:T(8,128)} %zroot.1, f32[1,512,1024]{2,1,0:T(8,128)} %panel_one.1, ...), custom_call_target="tpu_custom_call" | custom-call | tf_op jit(solution)/shard_map/pallas_call | solution.py:798
  169.5 3.3 %shard_map.130 = (f32[1,256]{1,0:T(1,128)}, f32[2,128]{1,0:T(2,128)}, f32[2,256,512]{2,1,0:T(8,128)}, f32[2,512,512]{2,1,0:T(8,128)}) custom-call(f32[1,256]{1,0:T(1,128)} %get-tuple-element.8.refs_0_, f32[2,128]{1,0:T(2,128)} %get-tuple-element.9.refs_1_, f32[2,256,512]{2,1,0:T(8,128)} %get-tuple-element.10.refs_2_, f32[2,512,512]{2,1,0:T(8,128)} %get-tuple-element.11.refs_3_), custom_call_target="tpu_custom_call" | custom-call | tf_op jit(solution)/shard_map/pallas_call | solution.py:849
where the time goes:
time: 173 us
  Pallas kernels  172 us (99%)
    pallas_call x1, Pallas kernels, line_body(): pl.pallas_call(line_kernel, out_shape=(jax.ShapeDtypeStruct((1, node), f3...  169 us

commit v1 on v0

--- a/solution.py
+++ b/solution.py
@@ -197,12 +197,15 @@
     beside,
     part_in,
     part_y,
+    cross_block,
     note,
     vec_a,
     vec_b,
     loads,
     note_send,
     note_recv,
+    x_send,
+    x_recv,
     line_send,
     line_recv,
     j_send,
@@ -546,12 +549,28 @@
 
         twice(go)
 
-    def gram(k):
-        columns = pl.ds(pl.multiple_of(r * node + k * STEP, STEP), STEP)
-        own[rows + k * STEP : rows + (k + 1) * STEP, :] = mm_t(chosen[0, :, columns], chosen[0]) + mm_t(
-            chosen[1, :, columns], chosen[1]
-        )
-        to_inner((steps + k) * per, (steps + k + 1) * per)
+    narrow = node // 2
+    thin = narrow * node // width
+    thick = node * node // width
+    left_core = 2 * side
+    others = (r, 2 - left_core, 3 - left_core)
+
+    def gram_block(down, along):
+        return mm_t(chosen[0, :, down], chosen[0, :, along]) + mm_t(chosen[1, :, down], chosen[1, :, along])
+
+    def gram_half():
+        along = pl.ds(pl.multiple_of((left_core + 1) * node + core * narrow, narrow), narrow)
+        block = gram_block(span(left_core, node), along)
+        for k in range(node // thin):
+            own[rows : rows + thin, k * narrow : (k + 1) * narrow] = block[k * thin : (k + 1) * thin, :]
+        to_inner(rows // PIECE, (rows + thin) // PIECE)
+
+    def gram(b):
+        block = gram_block(span(r, node), span(others[b], node))
+        first = rows + thin + b * thick
+        for k in range(node // thick):
+            own[first : first + thick, k * node : (k + 1) * node] = block[k * thick : (k + 1) * thick, :]
+        to_inner(first // PIECE, (first + thick) // PIECE)
 
     one = {}
 
@@ -601,14 +620,40 @@
         g_copy(k).wait_recv()
         g_copy(k + 1).start()
 
-    def node_step(step, m):
-        at = pl.ds(rows + step * STEP, STEP)
-        block = pick_rows(m, at)
-
-        def go(h):
-            z_j[m, step * STEP : (step + 1) * STEP, within(0, h)] = mm(block, full_j[:, within(m, h)])
-
-        twice(go)
+    def node_step(b, m):
+        first = rows + thin + b * thick
+        packed = pick_rows(m, pl.ds(first, thick))
+        block = jnp.concatenate([packed[:, k * node : (k + 1) * node] for k in range(node // thick)], 0)
+        part = mm(block, full_j[span(others[b], node), child(m)])
+        if b == 0:
+            z_j[m] = part
+        else:
+            z_j[m] += part
+
+    def x_copy():
+        place = cross_block.at[:, :, span(core, narrow)]
+        return remote(place, place, x_send, x_recv, at_row(twin))
+
+    def share_half():
+        for m in range(nodes):
+            packed = pick_rows(m, pl.ds(rows, thin))
+            block = jnp.concatenate([packed[:, k * narrow : (k + 1) * narrow] for k in range(node // thin)], 0)
+            cross_block[m, :, span(core, narrow)] = block
+        x_copy().start()
+
+    def twin_step():
+        x_copy().wait_recv()
+        beyond = span(twin, node)
+
+        @pl.when(core == 0)
+        def _():
+            for m in range(nodes):
+                z_j[m] += mm(cross_block[m], full_j[beyond, child(m)])
+
+        @pl.when(core == 1)
+        def _():
+            for m in range(nodes):
+                z_j[m] += mm_t(cross_block[m], full_j[beyond, child(m)])
 
     def upper(m, dest):
         return mm_t(chosen[m, :, span(dest, node)], z_r[m])
@@ -646,8 +691,10 @@
     work = {
         0: [item(separator_rows, 0)],
         1: [item(separator_rows, 1)],
-        2: [item(gram, 0)],
+        2: [gram_half],
+        3: [item(gram, 0)],
         4: [item(gram, 1)],
+        6: [item(gram, 2)],
         5: [square_sums],
         7: [gathered_j, item(reduce_part, 0, 0)],
         8: [item(reduce_part, 0, 1)],
@@ -671,18 +718,17 @@
         31: [item(reduce_part, 4, 0), item(reduce_part, 4, 1)],
         32: [item(root_wait, 2), item(root_step, 2, 0)],
         33: [item(root_step, 2, 1), item(gather_part, 3)],
+        34: [share_half],
         35: [item(gather_part, 4), item(root_wait, 3), item(root_wait, 4), item(root_step, 3, 0)],
         36: [item(upper_twin, 0)],
         37: [item(upper_over, 0), item(root_step, 3, 1)],
         38: [item(upper_twin, 1)],
         39: [item(upper_over, 1)],
-        40: [cross],
-        41: [item(node_step, 0, 0)],
-        42: [item(node_step, 0, 1)],
-        43: [item(upper_own, 0)],
-        44: [item(upper_own, 1)],
-        45: [level_one_out],
-        46: [separator_sums],
+        40: [item(node_step, 0, 0), item(node_step, 0, 1)],
+        41: [cross],
+        42: [twin_step, item(node_step, 1, 0), item(node_step, 1, 1)],
+        43: [item(upper_own, 0), item(upper_own, 1)],
+        44: [level_one_out, separator_sums],
     }
     done = 0
     for last in sorted(work) + [chunks - 1]:
@@ -701,7 +747,7 @@
 
     sums_r = one["sums_r"]
     for m in range(nodes):
-        node_step(1, m)
+        node_step(2, m)
     for m in range(nodes):
         u_copy(2 + m).wait_recv()
         z_j[m] = -(z_j[m] + part_in[m, node : 2 * node, :] + part_y[m])
@@ -736,6 +782,7 @@
 
         lax.fori_loop(chunks - RING, chunks, last, 0)
 
+    x_copy().wait_send()
     for k in range(3):
         j_copy(k).wait_send()
     for k in range(5):
@@ -788,7 +835,8 @@
     node = width // n
     nodes, two = inv_two.shape[:2]
     rows = zroot.shape[0]
-    chunks = (rows + node) // PIECE
+    height = rows + node - node // 2 * node // width
+    chunks = height // PIECE
     steps = rows // STEP
     f32 = jnp.float32
     smem = pl.BlockSpec(memory_space=pltpu.SMEM)
@@ -807,12 +855,12 @@
         out_specs=(vmem,) * 4,
         scratch_shapes=[
             pltpu.VMEM(zroot.shape, f32),
-            pltpu.VMEM((rows + node, width), f32),
+            pltpu.VMEM((height, width), f32),
             pltpu.VMEM((node, nodes * two), f32),
             pltpu.VMEM((rows, nodes * two), f32),
             pltpu.VMEM((nodes * 2 * node, two), f32),
             pltpu.VMEM((nodes * node, two), f32),
-            pltpu.VMEM((3, rows + node, width), f32),
+            pltpu.VMEM((3, height, width), f32),
             pltpu.VMEM((nodes, RING * PIECE, width), f32),
             pltpu.VMEM((width, nodes * two), f32),
             pltpu.VMEM((nodes, rows, width), f32),
@@ -821,10 +869,13 @@
             pltpu.VMEM((rows, width // 2), f32),
             pltpu.VMEM((nodes, 2 * node, two), f32),
             pltpu.VMEM((nodes, node, two), f32),
+            pltpu.VMEM((nodes, node, node), f32),
             pltpu.VMEM((2, 8, width), jnp.int32),
             pltpu.VMEM((4, width // 128, 128), f32),
             pltpu.VMEM((4, nodes * two // 128, 128), f32),
             dma((9,)),
+            dma,
+            dma,
             dma,
             dma,
             dma((5, chunks)),

time: 173 us -> 171 us (0.988)
  Pallas kernels: 172 us -> 170 us
    pallas_call x1, Pallas kernels: 169 us -> 167 us  [line_body(): pl.pallas_call(line_kernel, out_shape=(jax.ShapeDtypeStruct((1, node), f3...]
where the time goes in v1:
time: 171 us
  Pallas kernels  170 us (99%)
    pallas_call x1, Pallas kernels, line_body(): pl.pallas_call(line_kernel, out_shape=(jax.ShapeDtypeStruct((1, node), f3...  167 us

profile of v1, /device:TPU:0, one launch (start us, length us, event | category | flops | bytes accessed | tf_op | source)
XLA Modules:
  0.0 170.8 jit_solution(11743103351637919193)
XLA Ops:
  0.6 166.7 %shard_map.129 = (f32[1,256]{1,0:T(1,128)}, f32[2,128]{1,0:T(2,128)}, f32[2,256,512]{2,1,0:T(8,128)}, f32[2,512,512]{2,1,0:T(8,128)}) custom-call(s32[2]{0:T(128)} %parents.1, s32[2]{0:T(128)} %widths.1, s32[2,4]{1,0:T(2,128)} %tiles_j.1, s32[2,8]{1,0:T(2,128)} %tiles_r.1, f32[512,2048]{1,0:T(8,128)} %zroot.1, f32[1,512,1024]{2,1,0:T(8,128)} %panel_one.1, ...), custom_call_target="tpu_custom_call" | custom-call | tf_op jit(solution)/shard_map/pallas_call | solution.py:846
  167.3 3.3 %shard_map.130 = (f32[1,256]{1,0:T(1,128)}, f32[2,128]{1,0:T(2,128)}, f32[2,256,512]{2,1,0:T(8,128)}, f32[2,512,512]{2,1,0:T(8,128)}) custom-call(f32[1,256]{1,0:T(1,128)} %get-tuple-element.8.refs_0_, f32[2,128]{1,0:T(2,128)} %get-tuple-element.9.refs_1_, f32[2,256,512]{2,1,0:T(8,128)} %get-tuple-element.10.refs_2_, f32[2,512,512]{2,1,0:T(8,128)} %get-tuple-element.11.refs_3_), custom_call_target="tpu_custom_call" | custom-call | tf_op jit(solution)/shard_map/pallas_call | solution.py:900

commit v2 on v1

--- a/solution.py
+++ b/solution.py
@@ -181,6 +181,7 @@
     var_one,
     var_two,
     z_j,
+    z_out,
     z_r,
     root,
     own,
@@ -682,7 +683,11 @@
     def upper_own(m):
         part_in[m, node : 2 * node, :] = part_in[m, node : 2 * node, :] + upper(m, r)
 
+    def leave():
+        return pltpu.make_async_copy(z_r, z_out, loads.at[9])
+
     def separator_sums():
+        leave().start()
         one["sums_r"] = [colsum(near_r[:, child(m)], z_r[m]) for m in range(nodes)]
 
     def item(function, *arguments):
@@ -783,6 +788,7 @@
         lax.fori_loop(chunks - RING, chunks, last, 0)
 
     x_copy().wait_send()
+    leave().wait()
     for k in range(3):
         j_copy(k).wait_send()
     for k in range(5):
@@ -806,9 +812,19 @@
 
 def copy_kernel(*refs):
     sems = refs[-1]
-    order = (3, 2, 0, 1)
-    ins = [pltpu.make_async_copy(refs[k], refs[8 + k], sems.at[k]) for k in order]
-    outs = [pltpu.make_async_copy(refs[8 + k], refs[4 + k], sems.at[4 + k]) for k in order]
+    nodes, rows, _ = refs[3].shape
+    parts = [(3, (m, pl.ds(h * (rows // 2), rows // 2))) for m in range(nodes) for h in range(2)]
+    parts += [(2, (m,)) for m in range(nodes)] + [(0, ()), (1, ())]
+
+    def at(ref, place):
+        return ref.at[place] if place else ref
+
+    ins = []
+    outs = []
+    for i, (k, place) in enumerate(parts):
+        source, middle, target = (at(refs[k + 4 * d], place) for d in (0, 2, 1))
+        ins.append(pltpu.make_async_copy(source, middle, sems.at[i]))
+        outs.append(pltpu.make_async_copy(middle, target, sems.at[len(parts) + i]))
     for copy in ins:
         copy.start()
     for first, second in zip(ins, outs):
@@ -852,8 +868,9 @@
             jax.ShapeDtypeStruct((nodes, rows, two), f32),
         ),
         in_specs=[smem] * 4 + [hbm] * 6,
-        out_specs=(vmem,) * 4,
+        out_specs=(vmem, vmem, vmem, hbm),
         scratch_shapes=[
+            pltpu.VMEM((nodes, rows, two), f32),
             pltpu.VMEM(zroot.shape, f32),
             pltpu.VMEM((height, width), f32),
             pltpu.VMEM((node, nodes * two), f32),
@@ -873,7 +890,7 @@
             pltpu.VMEM((2, 8, width), jnp.int32),
             pltpu.VMEM((4, width // 128, 128), f32),
             pltpu.VMEM((4, nodes * two // 128, 128), f32),
-            dma((9,)),
+            dma((10,)),
             dma,
             dma,
             dma,
@@ -902,7 +919,7 @@
         out_shape=tuple(jax.ShapeDtypeStruct(one.shape, one.dtype) for one in results),
         in_specs=[hbm] * 4,
         out_specs=(hbm,) * 4,
-        scratch_shapes=[pltpu.VMEM(one.shape, one.dtype) for one in results] + [dma((8,))],
+        scratch_shapes=[pltpu.VMEM(one.shape, one.dtype) for one in results] + [dma((2 * (3 * nodes + 2),))],
         compiler_params=pltpu.CompilerParams(vmem_limit_bytes=60 * 1024 * 1024),
     )(*results)
 

time: 171 us -> 170 us (level)
  no operation moved by 1% of the time
where the time goes in v2:
time: 170 us
  Pallas kernels  169 us (99%)
    pallas_call x1, Pallas kernels, line_body(): pl.pallas_call(line_kernel, out_shape=(jax.ShapeDtypeStruct((1, node), f3...  166 us

profile of v2, /device:TPU:0, one launch (start us, length us, event | category | flops | bytes accessed | tf_op | source)
XLA Modules:
  0.0 169.7 jit_solution(7844762714876825139)
XLA Ops:
  0.6 166.0 %shard_map.129 = (f32[1,256]{1,0:T(1,128)}, f32[2,128]{1,0:T(2,128)}, f32[2,256,512]{2,1,0:T(8,128)}, f32[2,512,512]{2,1,0:T(8,128)}) custom-call(s32[2]{0:T(128)} %parents.1, s32[2]{0:T(128)} %widths.1, s32[2,4]{1,0:T(2,128)} %tiles_j.1, s32[2,8]{1,0:T(2,128)} %tiles_r.1, f32[512,2048]{1,0:T(8,128)} %zroot.1, f32[1,512,1024]{2,1,0:T(8,128)} %panel_one.1, ...), custom_call_target="tpu_custom_call" | custom-call | tf_op jit(solution)/shard_map/pallas_call | solution.py:862
  166.7 2.8 %shard_map.130 = (f32[1,256]{1,0:T(1,128)}, f32[2,128]{1,0:T(2,128)}, f32[2,256,512]{2,1,0:T(8,128)}, f32[2,512,512]{2,1,0:T(8,128)}) custom-call(f32[1,256]{1,0:T(1,128)} %get-tuple-element.8.refs_0_, f32[2,128]{1,0:T(2,128)} %get-tuple-element.9.refs_1_, f32[2,256,512]{2,1,0:T(8,128)} %get-tuple-element.10.refs_2_, f32[2,512,512]{2,1,0:T(8,128)} %get-tuple-element.11.refs_3_), custom_call_target="tpu_custom_call" | custom-call | tf_op jit(solution)/shard_map/pallas_call | solution.py:917

commit v3 on v2

--- a/solution.py
+++ b/solution.py
@@ -709,9 +709,9 @@
         15: [item(reduce_part, 1, 0)],
         16: [item(reduce_part, 1, 1)],
         17: [item(root_wait, 0), item(root_step, 0, 0)],
-        18: [item(root_step, 0, 1)],
+        18: [item(root_step, 0, 1), g_copy(2).start],
         19: [pair],
-        22: [item(pass_g, 0), item(gather_part, 1), g_copy(2).start],
+        22: [item(pass_g, 0), item(gather_part, 1)],
         23: [item(reduce_part, 2, 0)],
         24: [item(reduce_part, 2, 1)],
         25: [item(root_wait, 1), item(root_step, 1, 0)],

time: 170 us -> 170 us (level)
  no operation moved by 1% of the time
where the time goes in v3:
time: 170 us
  Pallas kernels  169 us (99%)
    pallas_call x1, Pallas kernels, line_body(): pl.pallas_call(line_kernel, out_shape=(jax.ShapeDtypeStruct((1, node), f3...  166 us

profile of v3, /device:TPU:0, one launch (start us, length us, event | category | flops | bytes accessed | tf_op | source)
XLA Modules:
  0.0 169.7 jit_solution(731491315608480410)
XLA Ops:
  0.6 166.0 %shard_map.129 = (f32[1,256]{1,0:T(1,128)}, f32[2,128]{1,0:T(2,128)}, f32[2,256,512]{2,1,0:T(8,128)}, f32[2,512,512]{2,1,0:T(8,128)}) custom-call(s32[2]{0:T(128)} %parents.1, s32[2]{0:T(128)} %widths.1, s32[2,4]{1,0:T(2,128)} %tiles_j.1, s32[2,8]{1,0:T(2,128)} %tiles_r.1, f32[512,2048]{1,0:T(8,128)} %zroot.1, f32[1,512,1024]{2,1,0:T(8,128)} %panel_one.1, ...), custom_call_target="tpu_custom_call" | custom-call | tf_op jit(solution)/shard_map/pallas_call | solution.py:862
  166.7 2.8 %shard_map.130 = (f32[1,256]{1,0:T(1,128)}, f32[2,128]{1,0:T(2,128)}, f32[2,256,512]{2,1,0:T(8,128)}, f32[2,512,512]{2,1,0:T(8,128)}) custom-call(f32[1,256]{1,0:T(1,128)} %get-tuple-element.8.refs_0_, f32[2,128]{1,0:T(2,128)} %get-tuple-element.9.refs_1_, f32[2,256,512]{2,1,0:T(8,128)} %get-tuple-element.10.refs_2_, f32[2,512,512]{2,1,0:T(8,128)} %get-tuple-element.11.refs_3_), custom_call_target="tpu_custom_call" | custom-call | tf_op jit(solution)/shard_map/pallas_call | solution.py:917
